TPU v7x, 128 devices: a whole 4x4x4 slice. The times are simulated.
128 devices in a mesh: dp: 4 (over y), expert: 32 (over x, z, core).
Axes of the slice: x: 4, y: 4, z: 4, core: 2. Of those that a mesh axis runs over, the one named last changes fastest.
Arguments:
- tokens: bfloat16 [16384, 2880], P(('dp', 'expert')), may hold values from -6 to 6
- cotangent: bfloat16 [16384, 2880], P(('dp', 'expert')), may hold values from -4 to 4
- route: int32 [16384, 4], P(('dp', 'expert')), may hold values from 0 to 63, all different within a row; in each aligned block of 128 rows (0 to 127, 128 to 255, ...) at most 16 rows name the same one
- combine: bfloat16 [16384, 4], P(('dp', 'expert')), may hold values from 0.049804688 to 0.59765625
- w_gate: bfloat16 [4, 32, 2880, 720], P('dp', 'expert'), may hold values from -0.109375 to 0.109375
- w_up: bfloat16 [4, 32, 2880, 720], P('dp', 'expert'), may hold values from -0.109375 to 0.109375
- w_down: bfloat16 [4, 32, 720, 2880], P('dp', 'expert'), may hold values from -0.15625 to 0.15625
Outputs:
- grad_tokens: bfloat16 [16384, 2880], P(('dp', 'expert'))
- grad_combine: float32 [16384, 4], P(('dp', 'expert'))
- grad_down: bfloat16 [4, 32, 720, 2880], P('dp', 'expert')
Inputs may be any that keep to these rules, and one draw needn't show every extreme that they name: `route`: each row names 4 different experts; every expert is named by some row. Among the rows of one device no expert is named more than 16 times, and in every draw some expert is named exactly 16 times by the rows of some device.
All inputs are finite; a program needn't handle non-finite values.
Results may differ from a plain program's by a relative error of at most 0.0058.
Values may be sent and summed in bfloat16 or wider, within the bound.
No kernel may reach another device: no remote copies, remote signals or barrier semaphores. Data moves between devices by JAX's collectives and lax.ppermute only.
A program may use at most 192 MiB of HBM per device.

v0:
```python
import jax
import jax.numpy as jnp
from jax import lax
from jax.sharding import PartitionSpec as P


def half_backward(rows, cot_rows, weight_rows, gate_half, up_half, down_half):
    contract = (((1,), (1,)), ((), ()))
    pre_gate = jnp.dot(rows, gate_half, preferred_element_type=jnp.float32)
    pre_up = jnp.dot(rows, up_half, preferred_element_type=jnp.float32)
    sigma = jax.nn.sigmoid(1.702 * pre_gate)
    act = (pre_gate * sigma * (pre_up + 1.0)).astype(jnp.bfloat16)
    act_wide = lax.optimization_barrier(act).astype(jnp.float32)
    back = lax.dot_general(cot_rows, down_half, contract, preferred_element_type=jnp.float32)
    partial_combine = jnp.sum(back * act_wide, axis=1).astype(jnp.bfloat16)
    weighted = weight_rows[:, None] * back
    grad_gate = (
        weighted * (pre_up + 1.0) * (sigma + 1.702 * pre_gate * sigma * (1.0 - sigma))
    ).astype(jnp.bfloat16)
    grad_up = (weighted * pre_gate * sigma).astype(jnp.bfloat16)
    partial_tokens = (
        lax.dot_general(grad_gate, gate_half, contract, preferred_element_type=jnp.float32)
        + lax.dot_general(grad_up, up_half, contract, preferred_element_type=jnp.float32)
    ).astype(jnp.bfloat16)
    scaled = (weight_rows[:, None] * cot_rows.astype(jnp.float32)).astype(jnp.bfloat16)
    return (partial_tokens, partial_combine, act, scaled)


def outer_sum(act, scaled):
    return lax.dot_general(
        act, scaled, (((0,), (0,)), ((), ())), preferred_element_type=jnp.float32
    )


def local(tokens, cotangent, route, combine, w_gate, w_up, w_down):
    dp_size = lax.axis_size("dp")
    col_size = lax.axis_size("expert")
    devices = dp_size * col_size
    tok_rows, feature = tokens.shape
    top_count = route.shape[1]
    experts_all = devices // 2
    pair_count = tok_rows * top_count
    capacity = 2 * pair_count // experts_all
    slot_total = devices * capacity
    gate_half = w_gate[0, 0]
    up_half = w_up[0, 0]
    down_half = w_down[0, 0]
    hidden_half = gate_half.shape[1]
    pair_expert = route.reshape(-1)
    onehot = (pair_expert[:, None] == jnp.arange(experts_all, dtype=jnp.int32)[None, :]).astype(
        jnp.int32
    )
    before = jnp.cumsum(onehot, axis=0, dtype=jnp.int32) - onehot
    slot_rank = jnp.sum(before * onehot, axis=1, dtype=jnp.int32)
    target = pair_expert * capacity + slot_rank
    token_of = jnp.arange(pair_count, dtype=jnp.int32) // top_count
    send_rows = (
        jnp.zeros((experts_all * capacity, feature), jnp.bfloat16).at[target].set(tokens[token_of])
    )
    send_cot = (
        jnp.zeros((experts_all * capacity, feature), jnp.bfloat16)
        .at[target]
        .set(cotangent[token_of])
    )
    send_weight = (
        jnp.zeros((experts_all * capacity,), jnp.bfloat16).at[target].set(combine.reshape(-1))
    )

    def spread(buffer):
        shaped = buffer.reshape((dp_size // 2, 1, col_size, capacity) + buffer.shape[1:])
        both = jnp.broadcast_to(shaped, (dp_size // 2, 2, col_size, capacity) + buffer.shape[1:])
        return both.reshape((slot_total,) + buffer.shape[1:])

    send_rows = spread(send_rows)
    send_cot = spread(send_cot)
    send_weight = spread(send_weight)
    got_rows, got_cot, got_weight = (
        lax.all_to_all(send_rows, ("dp", "expert"), split_axis=0, concat_axis=0, tiled=True),
        lax.all_to_all(send_cot, ("dp", "expert"), split_axis=0, concat_axis=0, tiled=True),
        lax.all_to_all(send_weight, ("dp", "expert"), split_axis=0, concat_axis=0, tiled=True),
    )
    living = (got_weight > 0).astype(jnp.int32)
    arrange = jnp.argsort(1 - living, stable=True)
    living_count = jnp.sum(living, dtype=jnp.int32)
    block_count = (living_count + 127) // 128
    rows_packed = got_rows[arrange]
    cot_packed = got_cot[arrange]
    weight_packed = got_weight[arrange].astype(jnp.float32)

    def one_block(block, carry):
        down_acc, token_acc, combine_acc = carry
        begin = block * 128
        rows = lax.dynamic_slice_in_dim(rows_packed, begin, 128, 0)
        cot_rows = lax.dynamic_slice_in_dim(cot_packed, begin, 128, 0)
        weight_rows = lax.dynamic_slice_in_dim(weight_packed, begin, 128, 0)
        partial_tokens, partial_combine, act, scaled = half_backward(
            rows, cot_rows, weight_rows, gate_half, up_half, down_half
        )
        down_acc = down_acc + outer_sum(act, scaled)
        token_acc = lax.dynamic_update_slice_in_dim(token_acc, partial_tokens, begin, 0)
        combine_acc = lax.dynamic_update_slice_in_dim(combine_acc, partial_combine, begin, 0)
        return (down_acc, token_acc, combine_acc)

    initial = (
        jnp.zeros((hidden_half, feature), jnp.float32),
        jnp.zeros((slot_total, feature), jnp.bfloat16),
        jnp.zeros((slot_total,), jnp.bfloat16),
    )
    down_total, packed_tokens, packed_combine = lax.fori_loop(0, block_count, one_block, initial)
    back_tokens = jnp.zeros_like(packed_tokens).at[arrange].set(packed_tokens)
    back_combine = jnp.zeros_like(packed_combine).at[arrange].set(packed_combine)
    returned_tokens, returned_combine = (
        lax.all_to_all(back_tokens, ("dp", "expert"), split_axis=0, concat_axis=0, tiled=True),
        lax.all_to_all(back_combine, ("dp", "expert"), split_axis=0, concat_axis=0, tiled=True),
    )
    dest_first = 2 * (pair_expert // col_size) * col_size + pair_expert % col_size
    first_row = dest_first * capacity + slot_rank
    second_row = (dest_first + col_size) * capacity + slot_rank
    token_terms = returned_tokens[first_row].astype(jnp.float32) + returned_tokens[
        second_row
    ].astype(jnp.float32)
    grad_tokens = jnp.sum(token_terms.reshape(tok_rows, top_count, feature), axis=1).astype(
        jnp.bfloat16
    )
    grad_combine = (
        returned_combine[first_row].astype(jnp.float32)
        + returned_combine[second_row].astype(jnp.float32)
    ).reshape(tok_rows, top_count)
    grad_down = down_total.astype(jnp.bfloat16).reshape(1, 1, hidden_half, feature)
    return (grad_tokens, grad_combine, grad_down)


def solution(mesh):
    in_specs = (
        P(("dp", "expert"), None),
        P(("dp", "expert"), None),
        P(("dp", "expert"), None),
        P(("dp", "expert"), None),
        P("dp", "expert", None, None),
        P("dp", "expert", None, None),
        P("dp", "expert", None, None),
    )
    out_specs = (
        P(("dp", "expert"), None),
        P(("dp", "expert"), None),
        P("dp", "expert", None, None),
    )
    return jax.shard_map(local, mesh=mesh, in_specs=in_specs, out_specs=out_specs, check_vma=False)
```

profile of v0, /device:TPU:34, one launch (start us, length us, event | category | flops | bytes accessed | tf_op | source)
XLA Modules:
  0.0 1016.3 jit_solution(16809786533350518789)
XLA Ops:
  5.4 3.8 scatter_custom_fusion
  10.3 10.5 %all-to-all-start = ((bf16[128,16,1]{1,2,0:T(2,128)(2,1)}), bf16[128,16,1]{1,2,0:T(2,128)(2,1)S(1)}, u32[]{:S(2)}, u32[]{:S(2)}) async-start(bf16[128,16,1]{1,2,0:T(2,128)(2,1)} %copy.47), calls=%async_computation | async-start | bytes 131072 | tf_op jit(solution)/shard_map/all_to_all | solution.py:80
  22.3 17.6 %scatter_custom_fusion.1 = bf16[1024,2880]{1,0:T(8,128)(2,1)} fusion(s32[512]{0:T(512)S(1)} %bitcast.77, bf16[128,2880]{1,0:T(8,128)(2,1)S(1)} %copy.48, s32[1024]{0:T(1024)S(1)} %pad_clamp_fusion.2, bf16[]{:T(256)} %constant.81.clone.1), kind=kCustom, calls=%fused_computation.53 | custom fusion | bytes 5898242 | tf_op jit(solution)/shard_map/scatter | solution.py:58
  39.9 8.0 broadcast_in_dim.26
  47.9 10.8 %all-to-all-start.1 = ((bf16[128,16,2880]{2,1,0:T(8,128)(2,1)}), bf16[128,16,2880]{2,1,0:T(8,128)(2,1)}, u32[]{:S(2)}, u32[]{:S(2)}) async-start(bf16[128,16,2880]{2,1,0:T(8,128)(2,1)} %bitcast.68), calls=%async_computation.1 | async-start | bytes 24117248 | tf_op jit(solution)/shard_map/all_to_all | solution.py:78
  59.0 17.6 %scatter_custom_fusion.2 = bf16[1024,2880]{1,0:T(8,128)(2,1)} fusion(s32[512]{0:T(512)S(1)} %bitcast.78, bf16[128,2880]{1,0:T(8,128)(2,1)S(1)} %copy.51, s32[1024]{0:T(1024)S(1)} %pad_clamp_fusion.2, bf16[]{:T(256)} %constant.81.clone.1), kind=kCustom, calls=%fused_computation.51 | custom fusion | bytes 5898242 | tf_op jit(solution)/shard_map/scatter | solution.py:63
  76.6 138.3 %all-to-all-done.1 = bf16[128,16,2880]{2,1,0:T(8,128)(2,1)} async-done(((bf16[128,16,2880]{2,1,0:T(8,128)(2,1)}), bf16[128,16,2880]{2,1,0:T(8,128)(2,1)}, u32[]{:S(2)}, u32[]{:S(2)}) %all-to-all-start.1) | async-done | bytes 11796512 | tf_op jit(solution)/shard_map/all_to_all | solution.py:78
  214.9 8.0 broadcast_in_dim.28
  223.0 9.4 all-to-all-start.2
  232.4 6.6 copy.49
  239.0 6.6 copy.50
  247.3 5.0 sort.17
  253.0 13.1 %gather_fusion.1 = bf16[2048]{0:T(1024)(128)(2,1)S(1)} fusion(bf16[2048]{0:T(1024)(128)(2,1)S(1)} %all_to_all.42, s32[2048]{0:T(1024)S(1)} %get-tuple-element.138), kind=kCustom, calls=%fused_computation.2 | custom fusion | bytes 16384 | tf_op jit(solution)/shard_map/gather | solution.py:88
  266.1 27.8 %gather_fusion = bf16[2048,2880]{1,0:T(8,128)(2,1)} fusion(bf16[2048,2880]{1,0:T(8,128)(2,1)} %bitcast.6, s32[2048]{0:T(1024)S(1)} %get-tuple-element.138), kind=kCustom, calls=%fused_computation.1 | custom fusion | bytes 23601152 | tf_op jit(solution)/shard_map/gather | solution.py:86
  293.9 94.8 %all-to-all-done.2 = bf16[128,16,2880]{2,1,0:T(8,128)(2,1)} async-done(((bf16[128,16,2880]{2,1,0:T(8,128)(2,1)}), bf16[128,16,2880]{2,1,0:T(8,128)(2,1)}, u32[]{:S(2)}, u32[]{:S(2)}) %all-to-all-start.2) | async-done | bytes 11796512 | tf_op jit(solution)/shard_map/all_to_all | solution.py:79
  388.6 27.8 %gather_fusion.2 = bf16[2048,2880]{1,0:T(8,128)(2,1)} fusion(bf16[2048,2880]{1,0:T(8,128)(2,1)} %bitcast.11, s32[2048]{0:T(1024)S(1)} %get-tuple-element.138), kind=kCustom, calls=%fused_computation.4 | custom fusion | bytes 23601152 | tf_op jit(solution)/shard_map/gather | solution.py:87
  416.5 3.9 broadcast_in_dim.24
  420.4 5.8 broadcast.310.clone
  426.2 158.4 %while.14 = (s32[]{:T(128)}, f32[720,2880]{1,0:T(8,128)}, bf16[2048,2880]{0,1:T(8,128)(2,1)}, bf16[2048]{0:T(1024)(128)(2,1)S(1)}, s32[]{:T(128)}, /*index=5*/bf...) while((s32[]{:T(128)}, f32[720,2880]{1,0:T(8,128)}, ...), condition=%wide.region_10.11_spmd, body=%wide.region_8.10_spmd.sunk | while | flops 3191823360 | bytes 154068656 | solution.py:109
  426.2 4.4 fusion.66
  430.7 4.5 multiply_convert_fusion.14
  435.2 2.7 convolution_add_fusion.4
  438.0 3.1 multiply_reduce_fusion.2
  446.0 4.4 fusion.66
  450.5 4.5 multiply_convert_fusion.14
  455.0 2.7 convolution_add_fusion.4
  457.8 3.1 multiply_reduce_fusion.2
  465.8 4.4 fusion.66
  470.2 4.5 multiply_convert_fusion.14
  474.8 2.7 convolution_add_fusion.4
  477.5 3.1 multiply_reduce_fusion.2
  485.5 4.4 fusion.66
  490.0 4.5 multiply_convert_fusion.14
  494.5 2.7 convolution_add_fusion.4
  497.3 3.1 multiply_reduce_fusion.2
  505.4 4.4 fusion.66
  509.8 4.5 multiply_convert_fusion.14
  514.4 2.7 convolution_add_fusion.4
  517.2 3.1 multiply_reduce_fusion.2
  525.2 4.4 fusion.66
  529.6 4.5 multiply_convert_fusion.14
  536.9 3.1 multiply_reduce_fusion.2
  544.9 4.4 fusion.66
  549.4 4.5 multiply_convert_fusion.14
  553.9 2.7 convolution_add_fusion.4
  556.7 3.1 multiply_reduce_fusion.2
  564.7 4.4 fusion.66
  569.2 4.5 multiply_convert_fusion.14
  573.7 2.7 convolution_add_fusion.4
  576.5 3.1 multiply_reduce_fusion.2
  584.6 14.7 %scatter_custom_fusion.4 = bf16[2048]{0:T(1024)(128)(2,1)S(1)} fusion(s32[2048]{0:T(1024)} %get-tuple-element.139, bf16[2048]{0:T(1024)(128)(2,1)S(1)} %get-tuple-element.66, bf16[]{:T(256)} %constant.81.clone.1), kind=kCustom, calls=%fused_computation.89 | custom fusion | bytes 4608 | tf_op jit(solution)/shard_map/scatter | solution.py:111
  600.0 161.7 %all-to-all-start.4 = ((bf16[128,16,1]{1,2,0:T(2,128)(2,1)}), bf16[128,16,1]{1,2,0:T(2,128)(2,1)S(1)}, u32[]{:S(2)}, u32[]{:S(2)}) async-start(bf16[128,16,1]{1,2,0:T(2,128)(2,1)} %all_to_all.55), calls=%async_computation.4 | async-start | bytes 131072 | tf_op jit(solution)/shard_map/all_to_all | solution.py:114
  761.8 16.4 %copy.53 = bf16[2048,2880]{1,0:T(8,128)(2,1)} copy(bf16[2048,2880]{0,1:T(8,128)(2,1)} %get-tuple-element.65) | data formatting | bytes 23592960 | tf_op jit(solution)/shard_map/while | solution.py:109
  778.1 24.5 %scatter_custom_fusion.3 = bf16[2048,2880]{1,0:T(8,128)(2,1)} fusion(s32[2048]{0:T(1024)} %get-tuple-element.139, bf16[2048,2880]{1,0:T(8,128)(2,1)} %copy.53, bf16[]{:T(256)} %constant.81.clone.1), kind=kCustom, calls=%fused_computation.48 | custom fusion | bytes 11796992 | tf_op jit(solution)/shard_map/scatter | solution.py:110
  802.7 10.2 %all-to-all-start.3 = ((bf16[128,16,2880]{2,1,0:T(8,128)(2,1)}), bf16[128,16,2880]{2,1,0:T(8,128)(2,1)}, u32[]{:S(2)}, u32[]{:S(2)}) async-start(bf16[128,16,2880]{2,1,0:T(8,128)(2,1)} %bitcast.67), calls=%async_computation.3 | async-start | bytes 24117248 | tf_op jit(solution)/shard_map/all_to_all | solution.py:113
  813.0 5.9 convert_bitcast_fusion
  819.1 3.5 gather_fusion.6
  822.6 3.5 gather_fusion.5
  826.9 144.0 %all-to-all-done.3 = bf16[128,16,2880]{2,1,0:T(8,128)(2,1)} async-done(((bf16[128,16,2880]{2,1,0:T(8,128)(2,1)}), bf16[128,16,2880]{2,1,0:T(8,128)(2,1)}, u32[]{:S(2)}, u32[]{:S(2)}) %all-to-all-start.3) | async-done | bytes 11796512 | tf_op jit(solution)/shard_map/all_to_all | solution.py:113
  970.9 11.8 %gather_fusion.4 = bf16[512,2880]{1,0:T(8,128)(2,1)S(1)} fusion(bf16[2048,2880]{1,0:T(8,128)(2,1)} %bitcast.14, s32[1024]{0:T(1024)S(1)} %pad_clamp_fusion), kind=kCustom, calls=%fused_computation.6 | custom fusion | bytes 5900288 | tf_op jit(solution)/shard_map/gather | solution.py:119
  982.7 12.7 %gather_fusion.3 = bf16[512,2880]{1,0:T(8,128)(2,1)} fusion(bf16[2048,2880]{1,0:T(8,128)(2,1)} %bitcast.14, s32[1024]{0:T(1024)S(1)} %pad_clamp_fusion.1), kind=kCustom, calls=%fused_computation.5 | custom fusion | bytes 5900288 | tf_op jit(solution)/shard_map/gather | solution.py:119
  995.5 5.0 convert_add_fusion
  1000.5 7.8 add.202
  1008.3 6.4 reduce_sum.41
  (237 shorter events, 54.2 us)
Async XLA Ops:
  10.3 29.6 %all-to-all-start = ((bf16[128,16,1]{1,2,0:T(2,128)(2,1)}), bf16[128,16,1]{1,2,0:T(2,128)(2,1)S(1)}, u32[]{:S(2)}, u32[]{:S(2)}) async-start(bf16[128,16,1]{1,2,0:T(2,128)(2,1)} %copy.47), calls=%async_computation | async-start | bytes 131072 | tf_op jit(solution)/shard_map/all_to_all | solution.py:80
  47.9 10.8 %copy-start.2 = (bf16[128,2880]{0,1:T(8,128)(2,1)S(1)}, bf16[128,2880]{0,1:T(8,128)(2,1)}, u32[]{:S(2)}) copy-start(bf16[128,2880]{0,1:T(8,128)(2,1)} %param.10) | copy-start | bytes 2211844
  47.9 167.1 %all-to-all-start.1 = ((bf16[128,16,2880]{2,1,0:T(8,128)(2,1)}), bf16[128,16,2880]{2,1,0:T(8,128)(2,1)}, u32[]{:S(2)}, u32[]{:S(2)}) async-start(bf16[128,16,2880]{2,1,0:T(8,128)(2,1)} %bitcast.68), calls=%async_computation.1 | async-start | bytes 24117248 | tf_op jit(solution)/shard_map/all_to_all | solution.py:78
  223.0 165.7 %all-to-all-start.2 = ((bf16[128,16,2880]{2,1,0:T(8,128)(2,1)}), bf16[128,16,2880]{2,1,0:T(8,128)(2,1)}, u32[]{:S(2)}, u32[]{:S(2)}) async-start(bf16[128,16,2880]{2,1,0:T(8,128)(2,1)} %bitcast.66), calls=%async_computation.2 | async-start | bytes 24117248 | tf_op jit(solution)/shard_map/all_to_all | solution.py:79
  426.2 9.0 copy-start
  430.7 7.3 slice-start.4
  430.7 10.5 %slice-start = ((s8[4423680]{0:T(1024)(128)(4,1)}), s8[4194304]{0:T(1024)(128)(4,1)S(1)}, s32[]{:S(2)}) async-start(s8[4423680]{0:T(1024)(128)(4,1)} %bitcast.58), calls=%async_computation.5 | async-start | bytes 8388608 | tf_op jit(solution)/shard_map/while
  435.2 2.7 slice-start.5
  435.2 5.9 slice-start.1
  437.9 4.7 copy-start.1
  438.0 5.5 slice-start.2
  446.0 9.0 copy-start
  450.4 7.3 slice-start.4
  450.4 10.5 %slice-start = ((s8[4423680]{0:T(1024)(128)(4,1)}), s8[4194304]{0:T(1024)(128)(4,1)S(1)}, s32[]{:S(2)}) async-start(s8[4423680]{0:T(1024)(128)(4,1)} %bitcast.58), calls=%async_computation.5 | async-start | bytes 8388608 | tf_op jit(solution)/shard_map/while
  455.0 2.7 slice-start.5
  455.0 5.9 slice-start.1
  457.7 4.7 copy-start.1
  457.7 5.5 slice-start.2
  465.8 9.0 copy-start
  470.2 7.3 slice-start.4
  470.2 10.5 %slice-start = ((s8[4423680]{0:T(1024)(128)(4,1)}), s8[4194304]{0:T(1024)(128)(4,1)S(1)}, s32[]{:S(2)}) async-start(s8[4423680]{0:T(1024)(128)(4,1)} %bitcast.58), calls=%async_computation.5 | async-start | bytes 8388608 | tf_op jit(solution)/shard_map/while
  474.8 2.7 slice-start.5
  474.8 5.9 slice-start.1
  477.5 4.7 copy-start.1
  477.5 5.5 slice-start.2
  485.5 9.0 copy-start
  490.0 7.3 slice-start.4
  490.0 10.5 %slice-start = ((s8[4423680]{0:T(1024)(128)(4,1)}), s8[4194304]{0:T(1024)(128)(4,1)S(1)}, s32[]{:S(2)}) async-start(s8[4423680]{0:T(1024)(128)(4,1)} %bitcast.58), calls=%async_computation.5 | async-start | bytes 8388608 | tf_op jit(solution)/shard_map/while
  494.5 2.7 slice-start.5
  494.5 5.9 slice-start.1
  497.3 4.7 copy-start.1
  497.3 5.5 slice-start.2
  505.4 9.0 copy-start
  509.8 7.3 slice-start.4
  509.8 10.5 %slice-start = ((s8[4423680]{0:T(1024)(128)(4,1)}), s8[4194304]{0:T(1024)(128)(4,1)S(1)}, s32[]{:S(2)}) async-start(s8[4423680]{0:T(1024)(128)(4,1)} %bitcast.58), calls=%async_computation.5 | async-start | bytes 8388608 | tf_op jit(solution)/shard_map/while
  514.4 2.7 slice-start.5
  514.4 5.9 slice-start.1
  517.1 4.7 copy-start.1
  517.1 5.5 slice-start.2
  525.2 9.0 copy-start
  529.6 7.3 slice-start.4
  529.6 10.5 %slice-start = ((s8[4423680]{0:T(1024)(128)(4,1)}), s8[4194304]{0:T(1024)(128)(4,1)S(1)}, s32[]{:S(2)}) async-start(s8[4423680]{0:T(1024)(128)(4,1)} %bitcast.58), calls=%async_computation.5 | async-start | bytes 8388608 | tf_op jit(solution)/shard_map/while
  534.2 5.9 slice-start.1
  536.9 4.7 copy-start.1
  536.9 5.5 slice-start.2
  544.9 9.0 copy-start
  549.4 7.3 slice-start.4
  549.4 10.5 %slice-start = ((s8[4423680]{0:T(1024)(128)(4,1)}), s8[4194304]{0:T(1024)(128)(4,1)S(1)}, s32[]{:S(2)}) async-start(s8[4423680]{0:T(1024)(128)(4,1)} %bitcast.58), calls=%async_computation.5 | async-start | bytes 8388608 | tf_op jit(solution)/shard_map/while
  553.9 2.7 slice-start.5
  553.9 5.9 slice-start.1
  556.6 4.7 copy-start.1
  556.7 5.5 slice-start.2
  564.7 9.0 copy-start
  569.1 7.3 slice-start.4
  569.1 10.5 %slice-start = ((s8[4423680]{0:T(1024)(128)(4,1)}), s8[4194304]{0:T(1024)(128)(4,1)S(1)}, s32[]{:S(2)}) async-start(s8[4423680]{0:T(1024)(128)(4,1)} %bitcast.58), calls=%async_computation.5 | async-start | bytes 8388608 | tf_op jit(solution)/shard_map/while
  573.7 2.7 slice-start.5
  573.7 5.9 slice-start.1
  576.4 4.7 copy-start.1
  576.5 5.5 slice-start.2
  600.0 202.6 %all-to-all-start.4 = ((bf16[128,16,1]{1,2,0:T(2,128)(2,1)}), bf16[128,16,1]{1,2,0:T(2,128)(2,1)S(1)}, u32[]{:S(2)}, u32[]{:S(2)}) async-start(bf16[128,16,1]{1,2,0:T(2,128)(2,1)} %all_to_all.55), calls=%async_computation.4 | async-start | bytes 131072 | tf_op jit(solution)/shard_map/all_to_all | solution.py:114
  802.7 10.2 %copy-start.4 = (s32[512]{0:T(512)S(1)}, s32[512]{0:T(512)}, u32[]{:S(2)}) copy-start(s32[512]{0:T(512)} %copy-done.3) | copy-start | bytes 6148
  802.7 10.2 %copy-start.6 = (s32[512,1]{0,1:T(1,128)S(1)}, s32[512,1]{0,1:T(1,128)}, u32[]{:S(2)}) copy-start(s32[512,1]{0,1:T(1,128)} %get-tuple-element.133) | copy-start | bytes 6148
  802.7 10.2 %copy-start.5 = (s32[512,1]{0,1:T(1,128)S(1)}, s32[512,1]{0,1:T(1,128)}, u32[]{:S(2)}) copy-start(s32[512,1]{0,1:T(1,128)} %get-tuple-element.132) | copy-start | bytes 6148
  802.7 168.2 %all-to-all-start.3 = ((bf16[128,16,2880]{2,1,0:T(8,128)(2,1)}), bf16[128,16,2880]{2,1,0:T(8,128)(2,1)}, u32[]{:S(2)}, u32[]{:S(2)}) async-start(bf16[128,16,2880]{2,1,0:T(8,128)(2,1)} %bitcast.67), calls=%async_computation.3 | async-start | bytes 24117248 | tf_op jit(solution)/shard_map/all_to_all | solution.py:113
  (10 other events, 21.6 us)
where the time goes:
time: 1020 us
  waiting for transfers between devices  377 us (37%)
  local copies, waits for them, and re-layouts  259 us (25%)
  starting transfers between devices  203 us (20%)
  matrix products  148 us (15%)
  other arithmetic  26.1 us (3%)
    all_to_all x1, starting transfers between devices, local(): lax.all_to_all(back_combine, ('dp', 'expert'), split_axis=0, concat_axis=...  162 us
    all_to_all x1, waiting for transfers between devices, local(): lax.all_to_all(back_tokens, ('dp', 'expert'), split_axis=0, concat_axis=0...  144 us
    all_to_all x1, waiting for transfers between devices, local(): lax.all_to_all(send_rows, ('dp', 'expert'), split_axis=0, concat_axis=0,...  138 us
    all_to_all x1, waiting for transfers between devices, local(): lax.all_to_all(send_cot, ('dp', 'expert'), split_axis=0, concat_axis=0, t...  94.8 us
    dot_general x8, matrix products, half_backward(): pre_up = jnp.dot(rows, up_half, preferred_element_type=jnp.float32)  35.7 us
    dot_general x8, matrix products, half_backward(): pre_gate = jnp.dot(rows, gate_half, preferred_element_type=jnp.float32)  35.6 us
    gather x1, local copies, waits for them, and re-layouts, local(): cot_packed = got_cot[arrange]  27.8 us
    gather x1, local copies, waits for them, and re-layouts, local(): rows_packed = got_rows[arrange]  27.8 us
  transfers between devices with their start and end apart: 5, of which 3 were waited for; matrix products, arithmetic and copies ran while one was open for 15% of the time, Pallas kernels for 0%

commit v1 on v0

v1 whole, which is shorter than its diff:
```python
import functools

import jax
import jax.numpy as jnp
from jax import lax
from jax.experimental import pallas as pl
from jax.experimental.pallas import tpu as pltpu
from jax.sharding import PartitionSpec as P

LANES = 128
VMEM_LIMIT = 60 * 1024 * 1024


def round_up(value, unit):
    return (value + unit - 1) // unit * unit


def slots_of(route, experts, capacity):
    rows = route.shape[0]
    hot = route[:, :, None] == jnp.arange(experts, dtype=jnp.int32)[None, None, :]
    named = jnp.any(hot, axis=1).astype(jnp.bfloat16)
    earlier = jnp.tril(jnp.ones((rows, rows), jnp.bfloat16), -1)
    before = jnp.dot(earlier, named, preferred_element_type=jnp.float32)
    rank = jnp.sum(jnp.where(hot, before[:, None, :], 0.0), axis=2).astype(jnp.int32)
    return route * capacity + rank


def select_kernel(first, count, slot_ref, rows_ref, extra_ref, out_ref):
    top = slot_ref.shape[0]
    width = rows_ref.shape[1]
    base = first + pl.program_id(0) * count
    place = base + lax.broadcasted_iota(jnp.int32, (count, slot_ref.shape[1]), 0)
    picks = [(slot_ref[c : c + 1, :] == place) for c in range(top)]
    pick = picks[0]
    for c in range(1, top):
        pick = jnp.logical_or(pick, picks[c])
    pick = pick.astype(jnp.float32).astype(jnp.bfloat16)
    body = jnp.dot(pick, rows_ref[...], preferred_element_type=jnp.float32)
    tail = body[:, width - LANES :]
    for c in range(top):
        one = picks[c].astype(jnp.float32).astype(jnp.bfloat16)
        tail += jnp.dot(one, extra_ref[c], preferred_element_type=jnp.float32)
    body = body.astype(jnp.bfloat16)
    tail = tail.astype(jnp.bfloat16)
    for h in range(out_ref.shape[1]):
        out_ref[0, h, :, : width - LANES] = body[:, : width - LANES]
        out_ref[0, h, :, width - LANES :] = tail


def select(slot, rows, extra, groups, halves, count):
    width = rows.shape[1]
    return pl.pallas_call(
        functools.partial(select_kernel, 0, count),
        grid=(groups,),
        out_shape=jax.ShapeDtypeStruct((groups, halves, count, width), jnp.bfloat16),
        in_specs=[
            pl.BlockSpec(slot.shape, lambda g: (0, 0)),
            pl.BlockSpec(rows.shape, lambda g: (0, 0)),
            pl.BlockSpec(extra.shape, lambda g: (0, 0, 0)),
        ],
        out_specs=pl.BlockSpec((1, halves, count, width), lambda g: (g, 0, 0, 0)),
        compiler_params=pltpu.CompilerParams(vmem_limit_bytes=VMEM_LIMIT),
        name="select_rows",
    )(slot, rows, extra)


def expert_kernel(spare, rows_ref, cot_ref, gate_ref, up_ref, down_ref, out_ref, act_ref):
    contract = (((1,), (1,)), ((), ()))
    width = rows_ref.shape[1]
    rows = rows_ref[...]
    pre_gate = jnp.dot(rows, gate_ref[...], preferred_element_type=jnp.float32)
    pre_up = jnp.dot(rows, up_ref[...], preferred_element_type=jnp.float32)
    back = lax.dot_general(
        cot_ref[...], down_ref[...], contract, preferred_element_type=jnp.float32
    )
    lane = lax.broadcasted_iota(jnp.int32, (rows.shape[0], LANES), 1)
    extra = jnp.where(lane >= spare, rows_ref[:, width - LANES :].astype(jnp.float32), 0.0)
    weight = jnp.sum(extra, axis=1, keepdims=True)
    sigma = jax.nn.sigmoid(1.702 * pre_gate)
    gated = pre_gate * sigma
    act = (gated * (pre_up + 1.0)).astype(jnp.bfloat16)
    act_ref[...] = act
    combine = jnp.sum(back * act.astype(jnp.float32), axis=1, keepdims=True)
    weighted = weight * back
    grad_gate = (
        weighted * (pre_up + 1.0) * (sigma + 1.702 * gated * (1.0 - sigma))
    ).astype(jnp.bfloat16)
    grad_up = (weighted * gated).astype(jnp.bfloat16)
    total = lax.dot_general(
        grad_gate, gate_ref[...], contract, preferred_element_type=jnp.float32
    ) + lax.dot_general(grad_up, up_ref[...], contract, preferred_element_type=jnp.float32)
    out_ref[:, : width - LANES] = total[:, : width - LANES].astype(jnp.bfloat16)
    tail = jnp.where(lane >= spare, jnp.where(extra > 0.0, combine, 0.0), total[:, width - LANES :])
    out_ref[:, width - LANES :] = tail.astype(jnp.bfloat16)


def expert_block(rows, cot, gate, up, down, spare, tile):
    count, width = rows.shape
    hidden = gate.shape[1]
    whole = lambda i: (0, 0)
    flops = 2 * 5 * count * width * hidden
    return pl.pallas_call(
        functools.partial(expert_kernel, spare),
        grid=(count // tile,),
        out_shape=(
            jax.ShapeDtypeStruct((count, width), jnp.bfloat16),
            jax.ShapeDtypeStruct((count, hidden), jnp.bfloat16),
        ),
        in_specs=[
            pl.BlockSpec((tile, width), lambda i: (i, 0)),
            pl.BlockSpec((tile, width), lambda i: (i, 0)),
            pl.BlockSpec(gate.shape, whole, pipeline_mode=pl.Buffered(1)),
            pl.BlockSpec(up.shape, whole, pipeline_mode=pl.Buffered(1)),
            pl.BlockSpec(down.shape, whole, pipeline_mode=pl.Buffered(1)),
        ],
        out_specs=(
            pl.BlockSpec((tile, width), lambda i: (i, 0)),
            pl.BlockSpec((tile, hidden), lambda i: (i, 0)),
        ),
        compiler_params=pltpu.CompilerParams(vmem_limit_bytes=VMEM_LIMIT),
        cost_estimate=pl.CostEstimate(
            flops=flops, bytes_accessed=6 * count * width + 6 * width * hidden, transcendentals=0
        ),
        name="expert_block",
    )(rows, cot, gate, up, down)


def down_kernel(spare, act_ref, tail_ref, cot_ref, out_ref, total_ref):
    step = pl.program_id(0)

    @pl.when(step == 0)
    def _():
        total_ref[...] = jnp.zeros_like(total_ref)

    lane = lax.broadcasted_iota(jnp.int32, tail_ref.shape, 1)
    extra = jnp.where(lane >= spare, tail_ref[...].astype(jnp.float32), 0.0)
    weight = jnp.sum(extra, axis=1, keepdims=True)
    scaled = (weight * cot_ref[...].astype(jnp.float32)).astype(jnp.bfloat16)
    total_ref[...] += lax.dot_general(
        act_ref[...], scaled, (((0,), (0,)), ((), ())), preferred_element_type=jnp.float32
    )

    @pl.when(step == pl.num_programs(0) - 1)
    def _():
        out_ref[...] = total_ref[: out_ref.shape[0], : out_ref.shape[1]].astype(jnp.bfloat16)


def down_block(act, rows, cot, spare, tile, hidden, feature):
    count, width = rows.shape
    padded = act.shape[1]
    return pl.pallas_call(
        functools.partial(down_kernel, spare),
        grid=(count // tile,),
        out_shape=jax.ShapeDtypeStruct((hidden, feature), jnp.bfloat16),
        in_specs=[
            pl.BlockSpec((tile, padded), lambda i: (i, 0)),
            pl.BlockSpec((tile, LANES), lambda i: (i, width // LANES - 1)),
            pl.BlockSpec((tile, width), lambda i: (i, 0)),
        ],
        out_specs=pl.BlockSpec((hidden, feature), lambda i: (0, 0)),
        scratch_shapes=[pltpu.VMEM((padded, width), jnp.float32)],
        compiler_params=pltpu.CompilerParams(vmem_limit_bytes=VMEM_LIMIT),
        cost_estimate=pl.CostEstimate(
            flops=2 * count * width * padded, bytes_accessed=2 * count * width, transcendentals=0
        ),
        name="down_block",
    )(act, rows, cot)


def gather_kernel(count, slot_ref, got_ref, token_ref, extra_ref, total_ref):
    step = pl.program_id(0)

    @pl.when(step == 0)
    def _():
        total_ref[...] = jnp.zeros_like(total_ref)

    top = slot_ref.shape[1]
    tokens = slot_ref.shape[0]
    width = got_ref.shape[2]
    base = step // 2 * count
    place = base + lax.broadcasted_iota(jnp.int32, (tokens, count), 1)
    pick = slot_ref[:, 0:1] == place
    for c in range(1, top):
        pick = jnp.logical_or(pick, slot_ref[:, c : c + 1] == place)
    pick = pick.astype(jnp.float32).astype(jnp.bfloat16)
    total_ref[...] += jnp.dot(pick, got_ref[0], preferred_element_type=jnp.float32)

    @pl.when(step == pl.num_programs(0) - 1)
    def _():
        token_ref[...] = total_ref[:, : token_ref.shape[1]].astype(jnp.bfloat16)
        extra_ref[...] = total_ref[:, width - LANES :]


def gather_sum(slot, got, feature):
    parts, count, width = got.shape
    tokens = slot.shape[0]
    return pl.pallas_call(
        functools.partial(gather_kernel, count),
        grid=(parts,),
        out_shape=(
            jax.ShapeDtypeStruct((tokens, feature), jnp.bfloat16),
            jax.ShapeDtypeStruct((tokens, LANES), jnp.float32),
        ),
        in_specs=[
            pl.BlockSpec(slot.shape, lambda i: (0, 0)),
            pl.BlockSpec((1, count, width), lambda i: (i, 0, 0)),
        ],
        out_specs=(
            pl.BlockSpec((tokens, feature), lambda i: (0, 0)),
            pl.BlockSpec((tokens, LANES), lambda i: (0, 0)),
        ),
        scratch_shapes=[pltpu.VMEM((tokens, width), jnp.float32)],
        compiler_params=pltpu.CompilerParams(vmem_limit_bytes=VMEM_LIMIT),
        name="gather_sum",
    )(slot, got)


def local(tokens, cotangent, route, combine, w_gate, w_up, w_down):
    dp_size = lax.axis_size("dp")
    col_size = lax.axis_size("expert")
    devices = dp_size * col_size
    tok_rows, feature = tokens.shape
    top = route.shape[1]
    experts = devices // 2
    capacity = 2 * tok_rows * top // experts
    hidden = w_gate.shape[3]
    width = round_up(feature + top, LANES)
    spare = feature - (width - LANES)
    wide = round_up(hidden, 256)
    gate = jnp.pad(w_gate[0, 0], ((0, width - feature), (0, wide - hidden)))
    up = jnp.pad(w_up[0, 0], ((0, width - feature), (0, wide - hidden)))
    down = jnp.pad(w_down[0, 0], ((0, wide - hidden), (0, width - feature)))
    slot = slots_of(route, experts, capacity)
    across = slot.T
    extra = jnp.zeros((top, tok_rows, LANES), jnp.bfloat16)
    for c in range(top):
        extra = extra.at[c, :, spare + c].set(combine[:, c])
    padding = ((0, 0), (0, width - feature))
    groups = dp_size // 2
    count = col_size * capacity

    def send(buffer):
        shaped = buffer.reshape(devices, capacity, width)
        got = lax.all_to_all(shaped, ("dp", "expert"), split_axis=0, concat_axis=0, tiled=True)
        return got.reshape(devices * capacity, width)

    rows = send(select(across, jnp.pad(tokens, padding), extra, groups, 2, count))
    cot = send(select(across, jnp.pad(cotangent, padding), jnp.zeros_like(extra), groups, 2, count))
    result, act = expert_block(rows, cot, gate, up, down, spare, 256)
    got = send(result)
    grad_down = down_block(act, rows, cot, spare, 512, hidden, feature)
    grad_tokens, tail = gather_sum(slot, got.reshape(dp_size, count, width), feature)
    grad_combine = tail[:, spare : spare + top]
    return grad_tokens, grad_combine, grad_down.reshape(1, 1, hidden, feature)


def solution(mesh):
    rows = P(("dp", "expert"), None)
    slab = P("dp", "expert", None, None)
    return jax.shard_map(
        local,
        mesh=mesh,
        in_specs=(rows, rows, rows, rows, slab, slab, slab),
        out_specs=(rows, rows, slab),
        check_vma=False,
    )
```

time: 1020 us -> 592 us (0.58)
  local copies, waits for them, and re-layouts: 259 us -> 36.9 us
  starting transfers between devices: 203 us -> 26.5 us
  matrix products: 148 us -> 0.2 us
  Pallas kernels: 0 us -> 95 us
  waiting for transfers between devices: 377 us -> 420 us
  other arithmetic: 26.1 us -> 6.84 us
    all_to_all x5 -> x3, starting transfers between devices: 203 us -> 26.5 us  [send(): lax.all_to_all(shaped, ('dp', 'expert'), split_axis=0, concat_axis=0, til...]
    dot_general x48 -> x1, matrix products: 148 us -> 0.2 us  [slots_of(): before = jnp.dot(earlier, named, preferred_element_type=jnp.float32)]
    gather x7 -> x0, local copies, waits for them, and re-layouts: 100 us -> none  [the longest x1 27.8 us: local(): cot_packed = got_cot[arrange]]
    pallas_call x0 -> x5, Pallas kernels: none -> 95 us  [the longest x1 58.2 us: expert_block(): pl.pallas_call(functools.partial(expert_kernel, spare), grid=(count // ti...]
    scatter x5 -> x4, local copies, waits for them, and re-layouts: 78.2 us -> 1.99 us  [local(): extra = extra.at[c, :, spare + c].set(combine[:, c])]
    all_to_all x5 -> x3, waiting for transfers between devices: 377 us -> 420 us  [send(): lax.all_to_all(shaped, ('dp', 'expert'), split_axis=0, concat_axis=0, til...]
    while x129 -> x0, local copies, waits for them, and re-layouts: 23.3 us -> none  [the longest x1 16.4 us: local(): lax.fori_loop(0, block_count, one_block, initial)]
    broadcast_in_dim x6 -> x0, local copies, waits for them, and re-layouts: 20.1 us -> none  [the longest x5 16.2 us: spread(): jnp.broadcast_to(shaped, (dp_size // 2, 2, col_size, capacity) + buffer.s...]
  transfers between devices with their start and end apart: 5 -> 3, of which waited for: 3 -> 3; matrix products, arithmetic and copies ran while one was open for 15% -> 4% of each run, Pallas kernels for 0% -> 4%
where the time goes in v1:
time: 592 us; the launch traced here: 586 us
  waiting for transfers between devices  420 us (71%)
  Pallas kernels  95 us (16%)
  local copies, waits for them, and re-layouts  36.9 us (6%)
  starting transfers between devices  26.5 us (4%)
  other arithmetic  6.84 us (1%)
    all_to_all x3, waiting for transfers between devices, send(): lax.all_to_all(shaped, ('dp', 'expert'), split_axis=0, concat_axis=0, til...  420 us
    pallas_call x1, Pallas kernels, expert_block(): pl.pallas_call(functools.partial(expert_kernel, spare), grid=(count // ti...  58.2 us
    all_to_all x3, starting transfers between devices, send(): lax.all_to_all(shaped, ('dp', 'expert'), split_axis=0, concat_axis=0, til...  26.5 us
    unnamed x20, local copies, waits for them, and re-layouts  19.5 us
    pallas_call x1, Pallas kernels, down_block(): pl.pallas_call(functools.partial(down_kernel, spare), grid=(count // tile...  16.3 us
    pallas_call x2, Pallas kernels, select(): pl.pallas_call(functools.partial(select_kernel, 0, count), grid=(groups,)...  13.2 us
  transfers between devices with their start and end apart: 3, of which 3 were waited for; matrix products, arithmetic and copies ran while one was open for 4% of the time, Pallas kernels for 4%

profile of v1, /device:TPU:34, one launch (start us, length us, event | category | flops | bytes accessed | tf_op | source)
XLA Modules:
  0.0 585.9 jit_solution(6194101132668846777)
XLA Ops:
  0.7 0.6 fusion.10
  1.3 2.6 and_reduce_fusion
  3.9 1.5 slice_bitcast_fusion
  5.4 0.1 copy.42
  5.5 0.1 copy.43
  5.7 0.1 copy.44
  5.8 0.1 copy.45
  5.9 0.7 fusion
  6.6 0.2 fusion.2
  6.8 0.7 select_reduce_fusion
  7.6 1.3 convert_add_fusion
  8.8 1.5 copy.41
  10.3 0.9 pad.30.rows_ref
  11.2 1.5 scatter.14
  12.7 0.2 scatter.15
  12.9 0.2 scatter.16
  13.1 0.2 scatter.19.extra_ref
  13.3 0.0 copy-start.1
  13.3 0.6 copy-done.1
  13.9 6.6 %select_rows.2 = bf16[2,2,512,2944]{3,2,1,0:T(8,128)(2,1)} custom-call(s32[4,128]{1,0:T(4,128)} %bitcast.32, bf16[128,2944]{1,0:T(8,128)(2,1)} %pad.30.rows_ref, bf16[4,128,128]{2,1,0:T(8,128)(2,1)} %copy-done.1), custom_call_target="tpu_custom_call" | custom-call | tf_op jit(solution)/shard_map/select_rows/pallas_call | solution.py:52
  20.5 0.0 copy-start
  20.5 10.6 %all-to-all-start = ((bf16[128,16,2944]{2,1,0:T(8,128)(2,1)}), bf16[128,16,2944]{2,1,0:T(8,128)(2,1)}, u32[]{:S(2)}, u32[]{:S(2)}) async-start(bf16[128,16,2944]{2,1,0:T(8,128)(2,1)} %bitcast.23), calls=%async_computation | async-start | bytes 24117248 | tf_op jit(solution)/shard_map/all_to_all | solution.py:244
  31.1 0.0 copy-done
  31.1 0.3 copy.46
  31.5 0.9 pad.31.rows_ref
  32.4 0.7 broadcast_1_extra_ref.2.extra_ref
  33.1 6.6 %select_rows.3 = bf16[2,2,512,2944]{3,2,1,0:T(8,128)(2,1)} custom-call(s32[4,128]{1,0:T(4,128)} %bitcast.33, bf16[128,2944]{1,0:T(8,128)(2,1)} %pad.31.rows_ref, bf16[4,128,128]{2,1,0:T(8,128)(2,1)} %broadcast_1_extra_ref.2.extra_ref), custom_call_target="tpu_custom_call" | custom-call | tf_op jit(solution)/shard_map/select_rows/pallas_call | solution.py:52
  39.7 149.5 %all-to-all-done = bf16[128,16,2944]{2,1,0:T(8,128)(2,1)} async-done(((bf16[128,16,2944]{2,1,0:T(8,128)(2,1)}), bf16[128,16,2944]{2,1,0:T(8,128)(2,1)}, u32[]{:S(2)}, u32[]{:S(2)}) %all-to-all-start) | async-done | bytes 12058656 | tf_op jit(solution)/shard_map/all_to_all | solution.py:244
  189.2 6.8 %all-to-all-start.1 = ((bf16[128,16,2944]{2,1,0:T(8,128)(2,1)}), bf16[128,16,2944]{2,1,0:T(8,128)(2,1)}, u32[]{:S(2)}, u32[]{:S(2)}) async-start(bf16[128,16,2944]{2,1,0:T(8,128)(2,1)} %bitcast.22), calls=%async_computation.1 | async-start | bytes 24117248 | tf_op jit(solution)/shard_map/all_to_all | solution.py:244
  196.0 6.5 %copy.47 = bf16[1,1,2880,720]{3,2,1,0:T(8,128)(2,1)} copy(bf16[1,1,2880,720]{2,3,1,0:T(8,128)(2,1)} %param.19) | data formatting | bytes 8294400 | tf_op args[4]
  202.5 6.6 %copy.48 = bf16[1,1,2880,720]{3,2,1,0:T(8,128)(2,1)} copy(bf16[1,1,2880,720]{2,3,1,0:T(8,128)(2,1)} %param.20) | data formatting | bytes 8294400 | tf_op args[5]
  209.1 0.0 slice-start
  209.1 0.0 slice-start.1
  209.1 4.9 pad.32.gate_ref
  214.0 0.0 slice-start.2
  214.0 0.0 slice-done
  214.0 0.0 slice-done.1
  214.0 0.0 slice-start.3
  214.0 2.8 pad.33.up_ref
  216.7 1.0 slice-done.2
  217.8 0.0 slice-done.3
  217.8 2.4 pad.34.down_ref
  220.2 133.2 %all-to-all-done.1 = bf16[128,16,2944]{2,1,0:T(8,128)(2,1)} async-done(((bf16[128,16,2944]{2,1,0:T(8,128)(2,1)}), bf16[128,16,2944]{2,1,0:T(8,128)(2,1)}, u32[]{:S(2)}, u32[]{:S(2)}) %all-to-all-start.1) | async-done | bytes 12058656 | tf_op jit(solution)/shard_map/all_to_all | solution.py:244
  353.4 58.2 %expert_block.1 = (bf16[2048,2944]{1,0:T(8,128)(2,1)}, bf16[2048,768]{1,0:T(8,128)(2,1)}) custom-call(bf16[2048,2944]{1,0:T(8,128)(2,1)} %bitcast.8.rows_ref.tail_ref, bf16[2048,2944]{1,0:T(8,128)(2,1)} %bitcast.10.cot_ref, bf16[2944,768]{1,0:T(8,128)(2,1)} %pad.32.gate_ref, bf16[2944,768]{1,0:T(8,128)(2,1)} %pad.33.up_ref, bf16[768,2944]{1,0:T(8,128)(2,1)} %pad.34.down_ref), custom_call_target="tpu_custom_call" | custom-call | flops 46305116160 | bytes 49741824 | tf_op jit(solution)/shard_map/expert_block/pallas_call | solution.py:102
  411.5 0.0 copy-start.2
  411.5 9.1 %all-to-all-start.2 = ((bf16[128,16,2944]{2,1,0:T(8,128)(2,1)}), bf16[128,16,2944]{2,1,0:T(8,128)(2,1)}, u32[]{:S(2)}, u32[]{:S(2)}) async-start(bf16[128,16,2944]{2,1,0:T(8,128)(2,1)} %bitcast.28), calls=%async_computation.2 | async-start | bytes 24117248 | tf_op jit(solution)/shard_map/all_to_all | solution.py:244
  420.7 0.0 copy-done.2
  420.7 0.7 copy.49.slot_ref
  421.4 16.3 %down_block.1 = bf16[720,2880]{1,0:T(8,128)(2,1)} custom-call(bf16[2048,768]{1,0:T(8,128)(2,1)} %get-tuple-element.58.act_ref, bf16[2048,2944]{1,0:T(8,128)(2,1)} %bitcast.8.rows_ref.tail_ref, bf16[2048,2944]{1,0:T(8,128)(2,1)} %bitcast.10.cot_ref), custom_call_target="tpu_custom_call" | custom-call | flops 9261023232 | bytes 12058624 | tf_op jit(solution)/shard_map/down_block/pallas_call | solution.py:151
  437.7 137.0 %all-to-all-done.2 = bf16[128,16,2944]{2,1,0:T(8,128)(2,1)} async-done(((bf16[128,16,2944]{2,1,0:T(8,128)(2,1)}), bf16[128,16,2944]{2,1,0:T(8,128)(2,1)}, u32[]{:S(2)}, u32[]{:S(2)}) %all-to-all-start.2) | async-done | bytes 12058656 | tf_op jit(solution)/shard_map/all_to_all | solution.py:244
  574.7 7.3 %gather_sum.1 = (bf16[128,2880]{1,0:T(8,128)(2,1)}, f32[128,128]{1,0:T(8,128)}) custom-call(s32[128,4]{1,0:T(8,128)} %copy.49.slot_ref, bf16[4,512,2944]{2,1,0:T(8,128)(2,1)} %bitcast.15.got_ref), custom_call_target="tpu_custom_call" | custom-call | tf_op jit(solution)/shard_map/gather_sum/pallas_call | solution.py:197
  582.1 2.3 copy.50
  584.3 0.9 slice.112
  585.2 0.7 copy.51
  (5 shorter events, 0.0 us)
Async XLA Ops:
  13.3 0.7 copy-start.1
  20.5 10.6 %copy-start = (bf16[128,2880]{0,1:T(8,128)(2,1)S(1)}, bf16[128,2880]{0,1:T(8,128)(2,1)}, u32[]{:S(2)}) copy-start(bf16[128,2880]{0,1:T(8,128)(2,1)} %param.16) | copy-start | bytes 2211844
  20.5 168.7 %all-to-all-start = ((bf16[128,16,2944]{2,1,0:T(8,128)(2,1)}), bf16[128,16,2944]{2,1,0:T(8,128)(2,1)}, u32[]{:S(2)}, u32[]{:S(2)}) async-start(bf16[128,16,2944]{2,1,0:T(8,128)(2,1)} %bitcast.23), calls=%async_computation | async-start | bytes 24117248 | tf_op jit(solution)/shard_map/all_to_all | solution.py:244
  189.2 164.2 %all-to-all-start.1 = ((bf16[128,16,2944]{2,1,0:T(8,128)(2,1)}), bf16[128,16,2944]{2,1,0:T(8,128)(2,1)}, u32[]{:S(2)}, u32[]{:S(2)}) async-start(bf16[128,16,2944]{2,1,0:T(8,128)(2,1)} %bitcast.22), calls=%async_computation.1 | async-start | bytes 24117248 | tf_op jit(solution)/shard_map/all_to_all | solution.py:244
  209.1 4.9 slice-start
  209.1 4.9 slice-start.1
  214.0 3.8 slice-start.2
  214.0 3.8 slice-start.3
  411.5 9.1 %copy-start.2 = (s32[128,4]{0,1:T(4,128)S(1)}, s32[128,4]{0,1:T(4,128)}, u32[]{:S(2)}) copy-start(s32[128,4]{0,1:T(4,128)} %convert_add_fusion) | copy-start | bytes 6148
  411.5 163.2 %all-to-all-start.2 = ((bf16[128,16,2944]{2,1,0:T(8,128)(2,1)}), bf16[128,16,2944]{2,1,0:T(8,128)(2,1)}, u32[]{:S(2)}, u32[]{:S(2)}) async-start(bf16[128,16,2944]{2,1,0:T(8,128)(2,1)} %bitcast.28), calls=%async_computation.2 | async-start | bytes 24117248 | tf_op jit(solution)/shard_map/all_to_all | solution.py:244
